TPU v7x, 128 devices: a whole 4x4x4 slice. The times are simulated.
128 devices in a mesh: row: 8 (over z, core), col: 8 (over x, y_hi), layer: 2 (over y_lo).
Axes of the slice: x: 4, y: 4 (y_hi: 2, y_lo: 2; y = y_hi * 2 + y_lo), z: 4, core: 2. Of those that a mesh axis runs over, the one named last changes fastest.
Arguments:
- stored_blocks: float32 [8, 8, 48, 128, 128], P('row', 'col'), as said below
- pattern: int32 [8, 8, 48], replicated, may hold values from -1 to 47, as said below
- result_cols: int32 [8, 8, 48, 2], P('row', 'col'), may hold values from 0 to 47, as said below
Outputs:
- result_blocks: float32 [8, 8, 48, 2, 128, 128], P('row', 'col', 'layer')
Inputs may be any that keep to these rules, and one draw needn't show every extreme that they name: Each block row of a tile holds at most one block. The pattern is symmetric: pattern(i, j, r) = c exactly when pattern(j, i, c) = r. Diagonal tiles hold just the diagonal blocks: pattern(i, i, r) = r. `result_cols`: the 2 columns listed for one block row of a tile are distinct. X is symmetric. stored_blocks(i, j, r) holds the block at local row r and local column pattern(i, j, r) of tile (i, j) when that block is upper; every other slot is zero.
All inputs are finite; a program needn't handle non-finite values.
Results may differ from a plain program's by a relative error of at most 0.0003.
Values sent between devices are 32-bit elements; how exact they have to be, the bound alone decides.
A program may use at most 128 MiB of HBM per device.

v0:
```python
import jax
import jax.numpy as jnp
from jax import lax
from jax.sharding import PartitionSpec as P


def shifted(value, axis, steps):
    count = lax.axis_size(axis)
    pairs = [(source, (source + steps) % count) for source in range(count)]
    return lax.ppermute(value, axis, pairs)


def accumulate(totals, left_tile, right_tile, left_cols, right_cols, wanted):
    inner_rows = jnp.maximum(left_cols, 0)
    partner = right_tile[inner_rows]
    target = right_cols[inner_rows]
    present = (left_cols >= 0) & (target >= 0)
    products = jnp.einsum(
        "rab,rbc->rac",
        left_tile,
        partner,
        precision=lax.Precision.HIGHEST,
        preferred_element_type=jnp.float32,
    )
    matched = (present[:, None] & (wanted == target[:, None])).astype(jnp.float32)
    return totals + matched[:, :, None, None] * products[:, None]


def complete(stored, mirror_source, pattern, tile_row, tile_col, grid_side):
    col_ids = pattern[tile_row, tile_col]
    safe_cols = jnp.maximum(col_ids, 0)
    local_rows = jnp.arange(stored.shape[0])
    is_upper = local_rows * grid_side + tile_row <= safe_cols * grid_side + tile_col
    mirrored = jnp.swapaxes(mirror_source[safe_cols], 1, 2)
    return jnp.where(is_upper[:, None, None], stored, mirrored)


def scatter_pieces(payload):
    return lax.all_to_all(payload, ("row", "col"), split_axis=1, concat_axis=1, tiled=True)


def collect_pieces(payload):
    return lax.all_to_all(payload, ("row", "col"), split_axis=1, concat_axis=1, tiled=True)


def per_device(stored_blocks, pattern, result_cols):
    grid_side = lax.axis_size("row")
    step_count = grid_side // lax.axis_size("layer")
    peer_count = grid_side * grid_side
    my_row = lax.axis_index("row")
    my_col = lax.axis_index("col")
    first_step = lax.axis_index("layer") * step_count
    own_tile = stored_blocks[0, 0]
    wanted = result_cols[0, 0]
    row_count = own_tile.shape[0]
    block_size = own_tile.shape[-1]
    piece_rows = block_size // peer_count
    held = scatter_pieces(own_tile.reshape(row_count, peer_count, 1, piece_rows, block_size))[
        :, :, 0
    ]
    destination = jnp.arange(peer_count, dtype=jnp.int32)
    dest_row = destination // grid_side
    dest_col = destination % grid_side
    inner_group = (dest_row + dest_col + first_step) % grid_side
    sources = jnp.stack(
        [
            dest_row * grid_side + inner_group,
            inner_group * grid_side + dest_row,
            inner_group * grid_side + dest_col,
            dest_col * grid_side + inner_group,
        ],
        axis=1,
    )
    arrived = collect_pieces(jnp.take(held, sources, axis=1))
    tiles = [
        arrived[:, :, number].reshape(row_count, block_size, block_size)
        for number in range(sources.shape[1])
    ]
    totals = jnp.zeros((row_count, wanted.shape[1], block_size, block_size), jnp.float32)
    middle = (my_row + my_col + first_step) % grid_side
    left_tile = complete(tiles[0], tiles[1], pattern, my_row, middle, grid_side)
    right_tile = complete(tiles[2], tiles[3], pattern, middle, my_col, grid_side)
    for step in range(step_count):
        totals = accumulate(
            totals, left_tile, right_tile, pattern[my_row, middle], pattern[middle, my_col], wanted
        )
        if step + 1 < step_count:
            left_tile = shifted(left_tile, "col", -1)
            right_tile = shifted(right_tile, "row", -1)
            middle = (middle + 1) % grid_side
    summed = lax.psum_scatter(totals, "layer", scatter_dimension=0, tiled=True)
    return summed[None, None]


def solution(mesh):
    return jax.shard_map(
        per_device,
        mesh=mesh,
        in_specs=(P("row", "col", None, None, None), P(), P("row", "col", None, None)),
        out_specs=P("row", "col", "layer", None, None, None),
        check_vma=False,
    )
```

profile of v0, /device:TPU:10, one launch (start us, length us, event | category | flops | bytes accessed | tf_op | source)
XLA Modules:
  0.0 634.0 jit_solution(9383065186835264429)
XLA Ops:
  6.5 5.4 copy.53
  11.9 10.6 %all-to-all-start = ((f32[48,64,1,2,128]{4,0,3,2,1:T(8,128)}), f32[48,64,1,2,128]{4,0,3,2,1:T(8,128)S(1)}, u32[]{:S(2)}, u32[]{:S(2)}) async-start(f32[48,64,1,2,128]{4,0,3,2,1:T(8,128)} %bitcast.69), calls=%async_computation | async-start | bytes 6291456 | tf_op jit(solution)/shard_map/all_to_all | solution.py:39
  23.0 41.6 %all-to-all-done = f32[48,64,1,2,128]{4,0,3,2,1:T(8,128)S(1)} async-done(((f32[48,64,1,2,128]{4,0,3,2,1:T(8,128)}), f32[48,64,1,2,128]{4,0,3,2,1:T(8,128)S(1)}, u32[]{:S(2)}, u32[]{:S(2)}) %all-to-all-start) | async-done | bytes 3145760 | tf_op jit(solution)/shard_map/all_to_all | solution.py:39
  64.6 5.9 gather_fusion.1
  70.4 10.0 %select_bitcast_fusion = f32[48,64,4,2,128]{4,0,3,2,1:T(8,128)} fusion(f32[64,4,48,2,128]{4,2,3,1,0:T(8,128)} %bitcast.67, pred[64,4]{1,0:T(8,128)(4,1)S(1)} %copy.52), kind=kLoop, calls=%fused_computation.11 | loop fusion | flops 3145728 | bytes 25166080 | tf_op jit(solution)/shard_map/jit(_take)/select_n | solution.py:74
  80.5 7.7 %all-to-all-start.1 = ((f32[48,64,4,2,128]{4,0,3,2,1:T(8,128)}), f32[48,64,4,2,128]{4,0,3,2,1:T(8,128)}, u32[]{:S(2)}, u32[]{:S(2)}) async-start(f32[48,64,4,2,128]{4,0,3,2,1:T(8,128)} %select_bitcast_fusion), calls=%async_computation.1 | async-start | bytes 25165824 | tf_op jit(solution)/shard_map/all_to_all | solution.py:43
  92.6 187.6 %all-to-all-done.1 = f32[48,64,4,2,128]{4,0,3,2,1:T(8,128)} async-done(((f32[48,64,4,2,128]{4,0,3,2,1:T(8,128)}), f32[48,64,4,2,128]{4,0,3,2,1:T(8,128)}, u32[]{:S(2)}, u32[]{:S(2)}) %all-to-all-start.1) | async-done | bytes 12582944 | tf_op jit(solution)/shard_map/all_to_all | solution.py:43
  280.2 8.6 %fusion.8 = (f32[48,64,1,2,128]{4,0,3,2,1:T(8,128)S(1)}, f32[48,64,1,2,128]{4,0,3,2,1:T(8,128)}, f32[48,64,1,2,128]{4,0,3,2,1:T(8,128)}, f32[48,64,1,2,128]{4,0,3,2,1:T(8,128)S(1)}) fusion(f32[48,64,4,2,128]{4,0,3,2,1:T(8,128)} %all-to-all-done.1), kind=kLoop, calls=%fused_computation.68 | loop fusion | bytes 25165824 | tf_op jit(solution)/shard_map/slice | solution.py:76
  295.7 5.2 copy.56
  312.0 4.5 gather_fusion.3
  321.1 4.5 collective-permute-start
  325.6 28.3 %collective-permute-done.1 = f32[48,128,128]{1,2,0:T(8,128)S(1)} collective-permute-done((f32[48,128,128]{1,2,0:T(8,128)S(1)}, f32[48,128,128]{1,2,0:T(8,128)S(1)}, u32[]{:S(2)}, u32[]{:S(2)}) %collective-permute-start.1) | collective-permute-done | bytes 3145760 | tf_op jit(solution)/shard_map/ppermute | solution.py:10
  357.1 35.1 %collective-permute-done = f32[48,128,128]{2,1,0:T(8,128)S(1)} collective-permute-done((f32[48,128,128]{2,1,0:T(8,128)S(1)}, f32[48,128,128]{2,1,0:T(8,128)S(1)}, u32[]{:S(2)}, u32[]{:S(2)}) %collective-permute-start) | collective-permute-done | bytes 3145760 | tf_op jit(solution)/shard_map/ppermute | solution.py:10
  392.3 4.9 collective-permute-start.2
  398.1 66.9 %collective-permute-done.2 = f32[48,128,128]{2,1,0:T(8,128)} collective-permute-done((f32[48,128,128]{2,1,0:T(8,128)S(1)}, f32[48,128,128]{2,1,0:T(8,128)}, u32[]{:S(2)}, u32[]{:S(2)}) %collective-permute-start.2) | collective-permute-done | bytes 3145760 | tf_op jit(solution)/shard_map/ppermute | solution.py:10
  465.0 5.0 collective-permute-start.4
  476.1 5.2 fusion.9
  489.2 7.7 %fusion.10 = f32[48,128,128]{2,1,0:T(8,128)} fusion(f32[48,128,128]{2,1,0:T(8,128)} %copy-done.8, f32[48,128,128]{2,1,0:T(8,128)} %gather_fusion.6), kind=kOutput, calls=%fused_computation.70 | convolution fusion | flops 1207959552 | bytes 9437184 | tf_op jit(solution)/shard_map/rab,rbc->rac/dot_general | solution.py:18
  500.4 4.3 gather_fusion.8
  504.8 7.7 %fusion.11 = f32[48,128,128]{2,1,0:T(8,128)} fusion(f32[48,128,128]{2,1,0:T(8,128)} %collective-permute-done.2, f32[48,128,128]{2,1,0:T(8,128)} %gather_fusion.8), kind=kOutput, calls=%fused_computation.71 | convolution fusion | flops 1207959552 | bytes 9437184 | tf_op jit(solution)/shard_map/rab,rbc->rac/dot_general | solution.py:18
  516.0 4.4 gather_fusion.10
  520.4 17.9 %collective-permute-done.4 = f32[48,128,128]{2,1,0:T(8,128)} collective-permute-done((f32[48,128,128]{2,1,0:T(8,128)}, f32[48,128,128]{2,1,0:T(8,128)}, u32[]{:S(2)}, u32[]{:S(2)}) %collective-permute-start.4) | collective-permute-done | bytes 3145760 | tf_op jit(solution)/shard_map/ppermute | solution.py:10
  538.3 5.3 fusion.12
  547.4 79.7 %reduce-scatter.2.cloned.1.call-done = f32[24,2,128,128]{3,2,1,0:T(8,128)} async-done(((f32[48,2,128,128]{3,2,1,0:T(8,128)}), f32[24,2,128,128]{3,2,1,0:T(8,128)}) %reduce-scatter.2.cloned.1.call-update) | async-done | bytes 3145744 | tf_op jit(solution)/shard_map/reduce_scatter | solution.py:91
  (69 shorter events, 56.3 us)
Async XLA Ops:
  11.9 52.6 %all-to-all-start = ((f32[48,64,1,2,128]{4,0,3,2,1:T(8,128)}), f32[48,64,1,2,128]{4,0,3,2,1:T(8,128)S(1)}, u32[]{:S(2)}, u32[]{:S(2)}) async-start(f32[48,64,1,2,128]{4,0,3,2,1:T(8,128)} %bitcast.69), calls=%async_computation | async-start | bytes 6291456 | tf_op jit(solution)/shard_map/all_to_all | solution.py:39
  80.5 199.7 %all-to-all-start.1 = ((f32[48,64,4,2,128]{4,0,3,2,1:T(8,128)}), f32[48,64,4,2,128]{4,0,3,2,1:T(8,128)}, u32[]{:S(2)}, u32[]{:S(2)}) async-start(f32[48,64,4,2,128]{4,0,3,2,1:T(8,128)} %select_bitcast_fusion), calls=%async_computation.1 | async-start | bytes 25165824 | tf_op jit(solution)/shard_map/all_to_all | solution.py:43
  88.2 539.0 %reduce-scatter.2.cloned.1.call-start = ((), (), s32[]{:S(2)}) async-start(), calls=%async_computation.3 | async-start | bytes 9437184 | tf_op jit(solution)/shard_map/reduce_scatter | solution.py:91
  312.0 4.5 copy-start.4
  316.5 2.8 copy-start.3
  316.5 4.3 copy-start.5
  319.1 2.1 copy-start.2
  319.1 34.8 %collective-permute-start.1 = (f32[48,128,128]{1,2,0:T(8,128)S(1)}, f32[48,128,128]{1,2,0:T(8,128)S(1)}, u32[]{:S(2)}, u32[]{:S(2)}) collective-permute-start(f32[48,128,128]{1,2,0:T(8,128)S(1)} %bitcast_select_fusion), channel_id=1, source_target_pairs={{0,112},{16,0},{32,16},{48,32},{64,48},{80,64},{96,80},{112,96},{1... | collective-permute-start | bytes 9437192 | tf_op jit(solution)/shard_map/ppermute | solution.py:10
  320.7 150.1 %copy-start.9 = (s32[1,1,48,2]{2,3,1,0:T(2,128)S(1)}, s32[1,1,48,2]{2,3,1,0:T(2,128)}, u32[]{:S(2)}) copy-start(s32[1,1,48,2]{2,3,1,0:T(2,128)} %param.5) | copy-start | bytes 1156
  321.1 32.7 %copy-start.6 = (f32[48,128,128]{2,1,0:T(8,128)}, f32[48,128,128]{2,1,0:T(8,128)S(1)}, u32[]{:S(2)}) copy-start(f32[48,128,128]{2,1,0:T(8,128)S(1)} %bitcast_select_fusion.1) | copy-start | bytes 9437188
  321.1 71.1 %collective-permute-start = (f32[48,128,128]{2,1,0:T(8,128)S(1)}, f32[48,128,128]{2,1,0:T(8,128)S(1)}, u32[]{:S(2)}, u32[]{:S(2)}) collective-permute-start(f32[48,128,128]{2,1,0:T(8,128)S(1)} %bitcast_select_fusion.1), channel_id=1, source_target_pairs={{0,14},{2,0},{4,2},{6,4},{8,6},{10,8},{12,10},{14,12},{1,15},{3,1}... | collective-permute-start | bytes 9437192 | tf_op jit(solution)/shard_map/ppermute | solution.py:10
  353.9 38.4 %copy-start.7 = (f32[48,128,128]{1,2,0:T(8,128)}, f32[48,128,128]{1,2,0:T(8,128)S(1)}, u32[]{:S(2)}) copy-start(f32[48,128,128]{1,2,0:T(8,128)S(1)} %collective-permute-done.1) | copy-start | bytes 9437188
  353.9 43.3 %collective-permute-start.3 = (f32[48,128,128]{1,2,0:T(8,128)S(1)}, f32[48,128,128]{1,2,0:T(8,128)}, u32[]{:S(2)}, u32[]{:S(2)}) collective-permute-start(f32[48,128,128]{1,2,0:T(8,128)S(1)} %collective-permute-done.1), channel_id=1, source_target_pairs={{0,112},{16,0},{32,16},{48,32},{64,48},{80,64},{96,80},{112,96},{1... | collective-permute-start | bytes 9437192 | tf_op jit(solution)/shard_map/ppermute | solution.py:10
  392.3 4.9 copy-start.8
  392.3 72.8 %collective-permute-start.2 = (f32[48,128,128]{2,1,0:T(8,128)S(1)}, f32[48,128,128]{2,1,0:T(8,128)}, u32[]{:S(2)}, u32[]{:S(2)}) collective-permute-start(f32[48,128,128]{2,1,0:T(8,128)S(1)} %collective-permute-done), channel_id=1, source_target_pairs={{0,14},{2,0},{4,2},{6,4},{8,6},{10,8},{12,10},{14,12},{1,15},{3,1}... | collective-permute-start | bytes 9437192 | tf_op jit(solution)/shard_map/ppermute | solution.py:10
  397.2 115.3 %collective-permute-start.5 = (f32[48,128,128]{1,2,0:T(8,128)}, f32[48,128,128]{1,2,0:T(8,128)}, u32[]{:S(2)}, u32[]{:S(2)}) collective-permute-start(f32[48,128,128]{1,2,0:T(8,128)} %collective-permute-done.3), channel_id=1, source_target_pairs={{0,112},{16,0},{32,16},{48,32},{64,48},{80,64},{96,80},{112,96},{1... | collective-permute-start | bytes 9437192 | tf_op jit(solution)/shard_map/ppermute | solution.py:10
  465.0 73.3 %collective-permute-start.4 = (f32[48,128,128]{2,1,0:T(8,128)}, f32[48,128,128]{2,1,0:T(8,128)}, u32[]{:S(2)}, u32[]{:S(2)}) collective-permute-start(f32[48,128,128]{2,1,0:T(8,128)} %collective-permute-done.2), channel_id=1, source_target_pairs={{0,14},{2,0},{4,2},{6,4},{8,6},{10,8},{12,10},{14,12},{1,15},{3,1}... | collective-permute-start | bytes 9437192 | tf_op jit(solution)/shard_map/ppermute | solution.py:10
  520.4 23.2 %copy-start = (f32[48,128,128]{2,1,0:T(8,128)S(1)}, f32[48,128,128]{2,1,0:T(8,128)}, u32[]{:S(2)}) copy-start(f32[48,128,128]{2,1,0:T(8,128)} %fusion.10) | copy-start | bytes 9437188
  520.4 23.2 %copy-start.1 = (f32[48,128,128]{2,1,0:T(8,128)S(1)}, f32[48,128,128]{2,1,0:T(8,128)}, u32[]{:S(2)}) copy-start(f32[48,128,128]{2,1,0:T(8,128)} %fusion.11) | copy-start | bytes 9437188
Sparse Core Ops, SparseCore 0:
  547.6 79.5 reduce-scatter.1
where the time goes:
time: 637 us; the launch traced here: 634 us
  waiting for transfers between devices  457 us (72%)
  local copies, waits for them, and re-layouts  81.5 us (13%)
  starting transfers between devices  37 us (6%)
  matrix products  25.9 us (4%)
  other arithmetic  18.6 us (3%)
  between operations  13.7 us (2%)
    all_to_all x1, waiting for transfers between devices, collect_pieces(): lax.all_to_all(payload, ('row', 'col'), split_axis=1, concat_axis=1, tile...  188 us
    ppermute x6, waiting for transfers between devices, shifted(): return lax.ppermute(value, axis, pairs)  148 us
    reduce_scatter x1, waiting for transfers between devices, per_device(): summed = lax.psum_scatter(totals, 'layer', scatter_dimension=0, tiled=True)  79.7 us
    all_to_all x1, waiting for transfers between devices, scatter_pieces(): lax.all_to_all(payload, ('row', 'col'), split_axis=1, concat_axis=1, tile...  41.6 us
    dot_general x4, matrix products, accumulate(): jnp.einsum('rab,rbc->rac', left_tile, partner, precision=lax.Precision.HI...  25.9 us
    slice x4, local copies, waits for them, and re-layouts, per_device(): arrived[:, :, number].reshape(row_count, block_size, block_size)  20.4 us
    ppermute x6, starting transfers between devices, shifted(): return lax.ppermute(value, axis, pairs)  18.5 us
    gather x4, local copies, waits for them, and re-layouts, accumulate(): partner = right_tile[inner_rows]  15.5 us
  transfers between devices with their start and end apart: 9, of which 7 were waited for; matrix products, arithmetic and copies ran while one was open for 9% of the time, Pallas kernels for 0%

commit v1 on v0

v1 whole, which is shorter than its diff:
```python
import functools

import jax
import jax.numpy as jnp
from jax import lax
from jax.experimental import pallas as pl
from jax.experimental.pallas import tpu as pltpu
from jax.sharding import PartitionSpec as P

MESH = pl.DeviceIdType.MESH
CHUNKS = 3


def product(a, b):
    a_hi = a.astype(jnp.bfloat16)
    a_lo = (a - a_hi.astype(jnp.float32)).astype(jnp.bfloat16)
    b_hi = b.astype(jnp.bfloat16)
    b_lo = (b - b_hi.astype(jnp.float32)).astype(jnp.bfloat16)
    left = jnp.concatenate([a_hi, a_lo, a_hi], axis=1)
    right = jnp.concatenate([b_hi, b_hi, b_lo], axis=0)
    return jnp.dot(left, right, preferred_element_type=jnp.float32)


def kernel(
    rows,
    pattern,
    wanted,
    stored,
    out,
    mirror_out,
    mirror_in,
    left,
    same0,
    same1,
    same2,
    same3,
    other0,
    other1,
    other2,
    other3,
    mirror_s,
    mirror_r,
    layer_s,
    layer_r,
    y_s,
    y_r,
    x_s,
    x_r,
    xf_s,
    xf_r,
    z_s,
    z_r,
    zf_s,
    zf_r,
    core_s,
    core_r,
):
    half = rows // 2
    step = half // CHUNKS
    row = lax.axis_index("row")
    col = lax.axis_index("col")
    lay = lax.axis_index("layer")
    z, k = row // 2, row % 2
    x, yh = col // 2, col % 2
    same = [same0, same1, same2, same3]
    other = [other0, other1, other2, other3]
    off_diagonal = row != col

    to_layer = {"layer": 1 - lay}
    to_y = {"col": 2 * x + (1 - yh)}
    to_core = {"row": 2 * z + (1 - k)}
    to_x = [{"col": (col + 2) % 8}, {"col": (col + 6) % 8}]
    to_z = [{"row": (row + 2) % 8}, {"row": (row + 6) % 8}]
    to_mirror = {"row": col, "col": row}

    barrier = pltpu.get_barrier_semaphore()
    for device in [to_layer, to_y, to_core, *to_x, *to_z]:
        pl.semaphore_signal(barrier, inc=1, device_id=device, device_id_type=MESH)

    @pl.when(off_diagonal)
    def _():
        pl.semaphore_signal(barrier, inc=1, device_id=to_mirror, device_id_type=MESH)

    def copy(source, target, send, recv, device):
        return pltpu.make_async_remote_copy(
            src_ref=source,
            dst_ref=target,
            send_sem=send,
            recv_sem=recv,
            device_id=device,
            device_id_type=MESH,
        )

    def part(h, ch):
        return pl.ds(h * half + ch * step, step)

    def piece(ch):
        return pl.ds(ch * step, step)

    def half_of(differs):
        return lay if differs == 0 else 1 - lay

    def mirror_copy(ch):
        return copy(mirror_out.at[piece(ch)], mirror_in.at[piece(ch)], mirror_s.at[ch], mirror_r.at[ch], to_mirror)

    def layer_copy(ch):
        at = part(lay, ch)
        return copy(same0.at[at], same0.at[at], layer_s.at[ch], layer_r.at[ch], to_layer)

    def y_copy(ch):
        return copy(left.at[0, piece(ch)], left.at[1, piece(ch)], y_s.at[ch], y_r.at[ch], to_y)

    def x_copy(way, s, ch):
        slot = (6 if way == 0 else 2) + s
        return copy(left.at[s, piece(ch)], left.at[slot, piece(ch)], x_s.at[way, s, ch], x_r.at[way, s, ch], to_x[way])

    def x_forward(way, ch):
        slot = 6 if way == 0 else 3
        return copy(left.at[slot, piece(ch)], left.at[4 + way, piece(ch)], xf_s.at[way, ch], xf_r.at[way, ch], to_x[way])

    def z_copy(way, d, ch):
        at = part(half_of(d), ch)
        target = same3 if way == 0 else same1
        return copy(same0.at[at], target.at[at], z_s.at[way, d, ch], z_r.at[way, d, ch], to_z[way])

    def z_forward(way, ch):
        at = part(half_of(way), ch)
        source = same3 if way == 0 else same1
        return copy(source.at[at], same2.at[at], zf_s.at[way, ch], zf_r.at[way, ch], to_z[way])

    def core_copy(dz, d, ch):
        at = part(half_of(d), ch)
        return copy(same[dz].at[at], other[dz].at[at], core_s.at[dz, d, ch], core_r.at[dz, d, ch], to_core)

    def each(body):
        def run(ch, carry):
            body(ch)
            return carry

        lax.fori_loop(0, CHUNKS, run, 0)

    pl.semaphore_wait(barrier, jnp.where(off_diagonal, 8, 7))

    @pl.when(off_diagonal)
    def _():
        def send_mirrored(ch):
            def pick(n, carry):
                at = ch * step + n
                source = pattern[(col * 8 + row) * rows + lay * half + at]
                mirror_out[at] = stored[jnp.maximum(source, 0)].T
                return carry

            lax.fori_loop(0, step, pick, 0)
            mirror_copy(ch).start()

        each(send_mirrored)

    def clear(n, carry):
        out[n] = jnp.zeros(out.shape[1:], out.dtype)
        return carry

    lax.fori_loop(0, half, clear, 0)

    def complete(ch):
        @pl.when(off_diagonal)
        def _():
            mirror_copy(ch).wait_recv()

            def choose(n, carry):
                at = ch * step + n
                r = lay * half + at
                c = jnp.maximum(pattern[(row * 8 + col) * rows + r], 0)
                upper = r * 8 + row <= c * 8 + col
                block = jnp.where(upper, stored[r], mirror_in[at])
                same0[r] = block
                left[0, at] = block
                return carry

            lax.fori_loop(0, step, choose, 0)

        @pl.when(jnp.logical_not(off_diagonal))
        def _():
            def take(n, carry):
                at = ch * step + n
                block = stored[lay * half + at]
                same0[lay * half + at] = block
                left[0, at] = block
                return carry

            lax.fori_loop(0, step, take, 0)

        layer_copy(ch).start()
        y_copy(ch).start()
        for way in range(2):
            x_copy(way, 0, ch).start()
            z_copy(way, 0, ch).start()
        core_copy(0, 0, ch).start()

    each(complete)

    def spread(ch):
        layer_copy(ch).wait_recv()
        for way in range(2):
            z_copy(way, 1, ch).start()
        core_copy(0, 1, ch).start()
        y_copy(ch).wait_recv()
        for way in range(2):
            x_copy(way, 1, ch).start()

    each(spread)

    def forward_first(ch):
        x_copy(0, 0, ch).wait_recv()
        x_forward(0, ch).start()
        z_copy(0, 0, ch).wait_recv()
        z_forward(0, ch).start()
        core_copy(3, 0, ch).start()
        z_copy(1, 0, ch).wait_recv()
        core_copy(1, 0, ch).start()

    each(forward_first)

    def forward_second(ch):
        x_copy(1, 1, ch).wait_recv()
        x_forward(1, ch).start()
        z_copy(1, 1, ch).wait_recv()
        z_forward(1, ch).start()
        core_copy(1, 1, ch).start()
        z_copy(0, 1, ch).wait_recv()
        core_copy(3, 1, ch).start()

    each(forward_second)

    def near(ch):
        x_copy(1, 0, ch).wait_recv()
        x_copy(0, 1, ch).wait_recv()
        for dz in (0, 1, 3):
            for d in range(2):
                core_copy(dz, d, ch).wait_recv()

    each(near)

    def multiply(dz, differs):
        tile = (other if differs else same)[dz]
        m = 2 * ((z + dz) % 4) + (k + differs) % 2
        slot = 2 * ((m // 2 + 4 - x) % 4) + (m % 2 + yh) % 2

        def one(n, carry):
            r = lay * half + n
            c = pattern[(row * 8 + m) * rows + r]
            inner = jnp.maximum(c, 0)
            t = pattern[(m * 8 + col) * rows + inner]
            present = jnp.logical_and(c >= 0, t >= 0)
            block = product(left[slot, n], tile[inner])
            for q in range(2):
                matched = jnp.logical_and(present, wanted[2 * r + q] == t)
                out[n, q] += block * jnp.where(matched, 1.0, 0.0)
            return carry

        lax.fori_loop(0, half, one, 0, unroll=4)

    def far(dz):
        return (z + dz - x + 4) % 4 == 2

    for dz in (0, 1, 3):
        @pl.when(jnp.logical_not(far(dz)))
        def _(dz=dz):
            multiply(dz, 0)
            multiply(dz, 1)

    def last(ch):
        for way in range(2):
            z_forward(way, ch).wait_recv()
            core_copy(2, way, ch).start()
            x_forward(way, ch).wait_recv()

    each(last)

    for dz in (0, 1, 3):
        @pl.when(far(dz))
        def _(dz=dz):
            multiply(dz, 0)
            multiply(dz, 1)

    multiply(2, 0)

    def last_core(ch):
        for d in range(2):
            core_copy(2, d, ch).wait_recv()

    each(last_core)
    multiply(2, 1)

    def drain(ch):
        @pl.when(off_diagonal)
        def _():
            mirror_copy(ch).wait_send()

        layer_copy(ch).wait_send()
        y_copy(ch).wait_send()
        for way in range(2):
            x_forward(way, ch).wait_send()
            z_forward(way, ch).wait_send()
            for d in range(2):
                x_copy(way, d, ch).wait_send()
                z_copy(way, d, ch).wait_send()
        for dz in range(4):
            for d in range(2):
                core_copy(dz, d, ch).wait_send()

    each(drain)


def per_device(stored_blocks, pattern, result_cols):
    tile = stored_blocks[0, 0]
    rows, size = tile.shape[0], tile.shape[-1]
    half = rows // 2
    vmem = pl.BlockSpec(memory_space=pltpu.VMEM)
    smem = pl.BlockSpec(memory_space=pltpu.SMEM)
    sems = pltpu.SemaphoreType.DMA
    block = (size, size)
    result = pl.pallas_call(
        functools.partial(kernel, rows),
        out_shape=jax.ShapeDtypeStruct((half, 2, *block), jnp.float32),
        in_specs=[smem, smem, vmem],
        out_specs=vmem,
        scratch_shapes=[
            pltpu.VMEM((half, *block), jnp.float32),
            pltpu.VMEM((half, *block), jnp.float32),
            pltpu.VMEM((8, half, *block), jnp.float32),
            *[pltpu.VMEM((rows, *block), jnp.float32)] * 8,
            *[sems((CHUNKS,))] * 6,
            *[sems((2, 2, CHUNKS))] * 2,
            *[sems((2, CHUNKS))] * 2,
            *[sems((2, 2, CHUNKS))] * 2,
            *[sems((2, CHUNKS))] * 2,
            *[sems((4, 2, CHUNKS))] * 2,
        ],
        compiler_params=pltpu.CompilerParams(
            collective_id=0, has_side_effects=True, vmem_limit_bytes=58 * 2**20
        ),
    )(pattern.reshape(-1), result_cols.reshape(-1), tile)
    return result[None, None]


def solution(mesh):
    return jax.shard_map(
        per_device,
        mesh=mesh,
        in_specs=(P("row", "col", None, None, None), P(), P("row", "col", None, None)),
        out_specs=P("row", "col", "layer", None, None, None),
        check_vma=False,
    )
```

time: 637 us -> 228 us (0.36)
  waiting for transfers between devices: 457 us -> 0 us
  Pallas kernels: 0 us -> 220 us
  local copies, waits for them, and re-layouts: 81.5 us -> 6.71 us
  starting transfers between devices: 37 us -> 0 us
  matrix products: 25.9 us -> 0 us
  other arithmetic: 18.6 us -> 0 us
  between operations: 13.7 us -> 0.01 us
    all_to_all x2 -> x0, waiting for transfers between devices: 229 us -> none  [the longest x1 188 us: collect_pieces(): lax.all_to_all(payload, ('row', 'col'), split_axis=1, concat_axis=1, tile...]
    pallas_call x0 -> x1, Pallas kernels: none -> 220 us  [per_device(): pl.pallas_call(functools.partial(kernel, rows), out_shape=jax.ShapeDtypeS...]
    ppermute x6 -> x0, waiting for transfers between devices: 148 us -> none  [shifted(): return lax.ppermute(value, axis, pairs)]
    reduce_scatter x1 -> x0, waiting for transfers between devices: 79.7 us -> none  [per_device(): summed = lax.psum_scatter(totals, 'layer', scatter_dimension=0, tiled=True)]
    gather x12 -> x0, local copies, waits for them, and re-layouts: 36.7 us -> none  [the longest x4 15.5 us: accumulate(): partner = right_tile[inner_rows]]
    dot_general x4 -> x0, matrix products: 25.9 us -> none  [accumulate(): jnp.einsum('rab,rbc->rac', left_tile, partner, precision=lax.Precision.HI...]
    slice x4 -> x0, local copies, waits for them, and re-layouts: 20.4 us -> none  [per_device(): arrived[:, :, number].reshape(row_count, block_size, block_size)]
    ppermute x6 -> x0, starting transfers between devices: 18.5 us -> none  [shifted(): return lax.ppermute(value, axis, pairs)]
  transfers between devices with their start and end apart: 9 -> 0, of which waited for: 7 -> 0; matrix products, arithmetic and copies ran while one was open for 9% -> 0% of each run, Pallas kernels for 0% -> 0%
where the time goes in v1:
time: 228 us; the launch traced here: 227 us
  Pallas kernels  220 us (96%)
  local copies, waits for them, and re-layouts  6.71 us (3%)
    pallas_call x1, Pallas kernels, per_device(): pl.pallas_call(functools.partial(kernel, rows), out_shape=jax.ShapeDtypeS...  220 us
    unnamed x2, local copies, waits for them, and re-layouts  4.67 us

profile of v1, /device:TPU:10, one launch (start us, length us, event | category | flops | bytes accessed | tf_op | source)
XLA Modules:
  0.0 227.1 jit_solution(394425225690629944)
XLA Ops:
  0.0 1.4 reshape.6.pattern
  1.4 0.8 copy.5
  2.2 0.6 reshape.7.wanted
  2.8 220.3 %shard_map.37 = f32[24,2,128,128]{3,2,1,0:T(8,128)} custom-call(s32[3072]{0:T(1024)} %reshape.6.pattern, s32[96]{0:T(128)} %reshape.7.wanted, f32[48,128,128]{2,1,0:T(8,128)} %bitcast.5), custom_call_target="tpu_custom_call" | custom-call | tf_op jit(solution)/shard_map/pallas_call | solution.py:322
  223.2 3.9 %copy.7 = f32[1,1,24,2,128,128]{5,4,3,2,1,0:T(8,128)} copy(f32[1,1,24,2,128,128]{5,4,3,2,1,0:T(8,128)} %bitcast.4) | data formatting | bytes 6291456

commit v2 on v1

--- a/solution.py
+++ b/solution.py
@@ -29,6 +29,8 @@
     out,
     mirror_out,
     mirror_in,
+    swapped,
+    passing,
     left,
     same0,
     same1,
@@ -40,6 +42,10 @@
     other3,
     mirror_s,
     mirror_r,
+    swap_s,
+    swap_r,
+    pass_s,
+    pass_r,
     layer_s,
     layer_r,
     y_s,
@@ -57,6 +63,7 @@
 ):
     half = rows // 2
     step = half // CHUNKS
+    sub = step // 2
     row = lax.axis_index("row")
     col = lax.axis_index("col")
     lay = lax.axis_index("layer")
@@ -64,22 +71,41 @@
     x, yh = col // 2, col % 2
     same = [same0, same1, same2, same3]
     other = [other0, other1, other2, other3]
-    off_diagonal = row != col
+    on_ring = x == z
+    crossed = k != yh
+    off_diagonal = jnp.logical_or(jnp.logical_not(on_ring), crossed)
 
     to_layer = {"layer": 1 - lay}
-    to_y = {"col": 2 * x + (1 - yh)}
+    to_y = {"col": 2 * x + (1 - yh), "layer": 1 - lay}
     to_core = {"row": 2 * z + (1 - k)}
     to_x = [{"col": (col + 2) % 8}, {"col": (col + 6) % 8}]
     to_z = [{"row": (row + 2) % 8}, {"row": (row + 6) % 8}]
-    to_mirror = {"row": col, "col": row}
+    to_straight = {"row": 2 * x + k, "col": 2 * z + yh}
+    to_crossed = {"row": 2 * z + yh, "col": 2 * x + k}
+    pass_out = {"row": 2 * x + yh, "col": 2 * x + k}
+    pass_in = {"row": row, "col": 2 * z + yh}
+    pass_from = [{"row": 2 * ((z + dz) % 4) + yh, "col": 2 * x + k} for dz in (1, 2, 3)]
+    pass_on = [{"row": row, "col": 2 * ((z + dz) % 4) + yh} for dz in (1, 2, 3)]
 
     barrier = pltpu.get_barrier_semaphore()
-    for device in [to_layer, to_y, to_core, *to_x, *to_z]:
-        pl.semaphore_signal(barrier, inc=1, device_id=device, device_id_type=MESH)
-
-    @pl.when(off_diagonal)
+
+    def greet(devices):
+        for device in devices:
+            pl.semaphore_signal(barrier, inc=1, device_id=device, device_id_type=MESH)
+
+    greet([to_layer, to_y, to_core, *to_x, *to_z])
+
+    @pl.when(crossed)
     def _():
-        pl.semaphore_signal(barrier, inc=1, device_id=to_mirror, device_id_type=MESH)
+        greet([to_crossed])
+
+    @pl.when(on_ring)
+    def _():
+        greet(pass_from + pass_on)
+
+    @pl.when(jnp.logical_not(on_ring))
+    def _():
+        greet([to_straight, pass_out, pass_in])
 
     def copy(source, target, send, recv, device):
         return pltpu.make_async_remote_copy(
@@ -100,15 +126,46 @@
     def half_of(differs):
         return lay if differs == 0 else 1 - lay
 
-    def mirror_copy(ch):
-        return copy(mirror_out.at[piece(ch)], mirror_in.at[piece(ch)], mirror_s.at[ch], mirror_r.at[ch], to_mirror)
+    def mirror_part(p, ch):
+        return pl.ds(ch * step + p * sub, sub)
+
+    def mirror_copy(p, ch, device):
+        at = mirror_part(p, ch)
+        return copy(mirror_out.at[at], mirror_in.at[at], mirror_s.at[p, ch], mirror_r.at[p, ch], device)
+
+    def swap_copy(ch):
+        at = pl.ds(ch * sub, sub)
+        return copy(mirror_out.at[mirror_part(0, ch)], swapped.at[at], mirror_s.at[0, ch], swap_r.at[ch], to_crossed)
+
+    def swap_on(ch):
+        at = pl.ds(ch * sub, sub)
+        return copy(swapped.at[at], mirror_in.at[mirror_part(0, ch)], swap_s.at[ch], mirror_r.at[0, ch], to_straight)
+
+    def pass_copy(ch):
+        at = pl.ds(ch * sub, sub)
+        slot = (z - x + 4) % 4 - 1
+        return copy(
+            mirror_out.at[mirror_part(1, ch)], passing.at[slot, at], mirror_s.at[1, ch], pass_r.at[slot, ch], pass_out
+        )
+
+    def passing_copy(slot, ch):
+        at = pl.ds(ch * sub, sub)
+        return copy(
+            passing.at[slot, at], mirror_in.at[mirror_part(1, ch)], pass_s.at[slot, ch], mirror_r.at[1, ch], pass_on[slot]
+        )
+
+    def arriving(slot, ch):
+        at = pl.ds(ch * sub, sub)
+        return copy(
+            mirror_out.at[mirror_part(1, ch)], passing.at[slot, at], mirror_s.at[1, ch], pass_r.at[slot, ch], pass_from[slot]
+        )
 
     def layer_copy(ch):
         at = part(lay, ch)
         return copy(same0.at[at], same0.at[at], layer_s.at[ch], layer_r.at[ch], to_layer)
 
     def y_copy(ch):
-        return copy(left.at[0, piece(ch)], left.at[1, piece(ch)], y_s.at[ch], y_r.at[ch], to_y)
+        return copy(same0.at[part(1 - lay, ch)], left.at[1, piece(ch)], y_s.at[ch], y_r.at[ch], to_y)
 
     def x_copy(way, s, ch):
         slot = (6 if way == 0 else 2) + s
@@ -139,20 +196,36 @@
 
         lax.fori_loop(0, CHUNKS, run, 0)
 
-    pl.semaphore_wait(barrier, jnp.where(off_diagonal, 8, 7))
+    pl.semaphore_wait(barrier, 7 + jnp.where(on_ring, 6, 3) + jnp.where(crossed, 1, 0))
+
+    def send_mirrored(ch):
+        def pick(n, carry):
+            at = ch * step + n
+            source = pattern[col, row, lay * half + at]
+            mirror_out[at] = stored[jnp.maximum(source, 0)].T
+            return carry
+
+        lax.fori_loop(0, step, pick, 0)
+
+        @pl.when(on_ring)
+        def _():
+            mirror_copy(0, ch, to_crossed).start()
+            mirror_copy(1, ch, to_crossed).start()
+
+        @pl.when(jnp.logical_not(on_ring))
+        def _():
+            @pl.when(crossed)
+            def _():
+                swap_copy(ch).start()
+
+            @pl.when(jnp.logical_not(crossed))
+            def _():
+                mirror_copy(0, ch, to_straight).start()
+
+            pass_copy(ch).start()
 
     @pl.when(off_diagonal)
     def _():
-        def send_mirrored(ch):
-            def pick(n, carry):
-                at = ch * step + n
-                source = pattern[(col * 8 + row) * rows + lay * half + at]
-                mirror_out[at] = stored[jnp.maximum(source, 0)].T
-                return carry
-
-            lax.fori_loop(0, step, pick, 0)
-            mirror_copy(ch).start()
-
         each(send_mirrored)
 
     def clear(n, carry):
@@ -161,15 +234,24 @@
 
     lax.fori_loop(0, half, clear, 0)
 
+    def straight_on(ch):
+        swap_copy(ch).wait_recv()
+        swap_on(ch).start()
+
+    @pl.when(jnp.logical_and(crossed, jnp.logical_not(on_ring)))
+    def _():
+        each(straight_on)
+
     def complete(ch):
         @pl.when(off_diagonal)
         def _():
-            mirror_copy(ch).wait_recv()
+            mirror_copy(0, ch, to_straight).wait_recv()
+            mirror_copy(1, ch, to_straight).wait_recv()
 
             def choose(n, carry):
                 at = ch * step + n
                 r = lay * half + at
-                c = jnp.maximum(pattern[(row * 8 + col) * rows + r], 0)
+                c = jnp.maximum(pattern[row, col, r], 0)
                 upper = r * 8 + row <= c * 8 + col
                 block = jnp.where(upper, stored[r], mirror_in[at])
                 same0[r] = block
@@ -190,16 +272,22 @@
             lax.fori_loop(0, step, take, 0)
 
         layer_copy(ch).start()
-        y_copy(ch).start()
         for way in range(2):
             x_copy(way, 0, ch).start()
             z_copy(way, 0, ch).start()
         core_copy(0, 0, ch).start()
 
+        @pl.when(on_ring)
+        def _():
+            for slot in range(3):
+                arriving(slot, ch).wait_recv()
+                passing_copy(slot, ch).start()
+
     each(complete)
 
     def spread(ch):
         layer_copy(ch).wait_recv()
+        y_copy(ch).start()
         for way in range(2):
             z_copy(way, 1, ch).start()
         core_copy(0, 1, ch).start()
@@ -247,13 +335,13 @@
 
         def one(n, carry):
             r = lay * half + n
-            c = pattern[(row * 8 + m) * rows + r]
+            c = pattern[row, m, r]
             inner = jnp.maximum(c, 0)
-            t = pattern[(m * 8 + col) * rows + inner]
+            t = pattern[m, col, inner]
             present = jnp.logical_and(c >= 0, t >= 0)
             block = product(left[slot, n], tile[inner])
             for q in range(2):
-                matched = jnp.logical_and(present, wanted[2 * r + q] == t)
+                matched = jnp.logical_and(present, wanted[q, r] == t)
                 out[n, q] += block * jnp.where(matched, 1.0, 0.0)
             return carry
 
@@ -294,7 +382,17 @@
     def drain(ch):
         @pl.when(off_diagonal)
         def _():
-            mirror_copy(ch).wait_send()
+            mirror_copy(0, ch, to_straight).wait_send()
+            mirror_copy(1, ch, to_straight).wait_send()
+
+        @pl.when(jnp.logical_and(crossed, jnp.logical_not(on_ring)))
+        def _():
+            swap_on(ch).wait_send()
+
+        @pl.when(on_ring)
+        def _():
+            for slot in range(3):
+                passing_copy(slot, ch).wait_send()
 
         layer_copy(ch).wait_send()
         y_copy(ch).wait_send()
@@ -327,9 +425,14 @@
         scratch_shapes=[
             pltpu.VMEM((half, *block), jnp.float32),
             pltpu.VMEM((half, *block), jnp.float32),
+            pltpu.VMEM((half // 2, *block), jnp.float32),
+            pltpu.VMEM((3, half // 2, *block), jnp.float32),
             pltpu.VMEM((8, half, *block), jnp.float32),
             *[pltpu.VMEM((rows, *block), jnp.float32)] * 8,
-            *[sems((CHUNKS,))] * 6,
+            *[sems((2, CHUNKS))] * 2,
+            *[sems((CHUNKS,))] * 2,
+            *[sems((3, CHUNKS))] * 2,
+            *[sems((CHUNKS,))] * 4,
             *[sems((2, 2, CHUNKS))] * 2,
             *[sems((2, CHUNKS))] * 2,
             *[sems((2, 2, CHUNKS))] * 2,
@@ -339,7 +442,7 @@
         compiler_params=pltpu.CompilerParams(
             collective_id=0, has_side_effects=True, vmem_limit_bytes=58 * 2**20
         ),
-    )(pattern.reshape(-1), result_cols.reshape(-1), tile)
+    )(pattern, result_cols[0, 0].T, tile)
     return result[None, None]
 
 

time: 228 us -> 192 us (0.84)
  the two profiles are of different devices: /device:TPU:10 before, /device:TPU:38 now
where the time goes in v2:
time: 192 us
  Pallas kernels  188 us (98%)
  local copies, waits for them, and re-layouts  3.91 us (2%)
    pallas_call x1, Pallas kernels, per_device(): pl.pallas_call(functools.partial(kernel, rows), out_shape=jax.ShapeDtypeS...  188 us
    unnamed x1, local copies, waits for them, and re-layouts  3.91 us

profile of v2, /device:TPU:38, one launch (start us, length us, event | category | flops | bytes accessed | tf_op | source)
XLA Modules:
  0.0 191.7 jit_solution(9197227207252767723)
XLA Ops:
  0.0 187.8 %shard_map.37 = f32[24,2,128,128]{3,2,1,0:T(8,128)} custom-call(s32[8,8,48]{2,1,0:T(8,128)} %pattern.1, s32[2,48]{1,0:T(2,128)} %bitcast.7, f32[48,128,128]{2,1,0:T(8,128)} %bitcast.6), custom_call_target="tpu_custom_call" | custom-call | tf_op jit(solution)/shard_map/pallas_call | solution.py:420
  187.8 3.9 %copy.5 = f32[1,1,24,2,128,128]{5,4,3,2,1,0:T(8,128)} copy(f32[1,1,24,2,128,128]{5,4,3,2,1,0:T(8,128)} %bitcast.5) | data formatting | bytes 6291456

commit v3 on v2

--- a/solution.py
+++ b/solution.py
@@ -8,7 +8,7 @@
 from jax.sharding import PartitionSpec as P
 
 MESH = pl.DeviceIdType.MESH
-CHUNKS = 3
+CHUNKS = 4
 
 
 def product(a, b):
@@ -242,6 +242,15 @@
     def _():
         each(straight_on)
 
+    def pass_along(ch):
+        for slot in range(3):
+            arriving(slot, ch).wait_recv()
+            passing_copy(slot, ch).start()
+
+    @pl.when(on_ring)
+    def _():
+        each(pass_along)
+
     def complete(ch):
         @pl.when(off_diagonal)
         def _():
@@ -276,12 +285,6 @@
             x_copy(way, 0, ch).start()
             z_copy(way, 0, ch).start()
         core_copy(0, 0, ch).start()
-
-        @pl.when(on_ring)
-        def _():
-            for slot in range(3):
-                arriving(slot, ch).wait_recv()
-                passing_copy(slot, ch).start()
 
     each(complete)
 

time: 192 us -> 172 us (0.90)
  the two profiles are of different devices: /device:TPU:38 before, /device:TPU:40 now
where the time goes in v3:
time: 172 us
  Pallas kernels  168 us (98%)
  local copies, waits for them, and re-layouts  3.91 us (2%)
    pallas_call x1, Pallas kernels, per_device(): pl.pallas_call(functools.partial(kernel, rows), out_shape=jax.ShapeDtypeS...  168 us
    unnamed x1, local copies, waits for them, and re-layouts  3.91 us

profile of v3, /device:TPU:40, one launch (start us, length us, event | category | flops | bytes accessed | tf_op | source)
XLA Modules:
  0.0 172.3 jit_solution(7225265272769942876)
XLA Ops:
  0.0 168.4 %shard_map.37 = f32[24,2,128,128]{3,2,1,0:T(8,128)} custom-call(s32[8,8,48]{2,1,0:T(8,128)} %pattern.1, s32[2,48]{1,0:T(2,128)} %bitcast.7, f32[48,128,128]{2,1,0:T(8,128)} %bitcast.6), custom_call_target="tpu_custom_call" | custom-call | tf_op jit(solution)/shard_map/pallas_call | solution.py:423
  168.4 3.9 %copy.5 = f32[1,1,24,2,128,128]{5,4,3,2,1,0:T(8,128)} copy(f32[1,1,24,2,128,128]{5,4,3,2,1,0:T(8,128)} %bitcast.5) | data formatting | bytes 6291456

commit v4 on v3

--- a/solution.py
+++ b/solution.py
@@ -9,6 +9,7 @@
 
 MESH = pl.DeviceIdType.MESH
 CHUNKS = 4
+SIDE = 0
 
 
 def product(a, b):
@@ -86,6 +87,14 @@
     pass_in = {"row": row, "col": 2 * z + yh}
     pass_from = [{"row": 2 * ((z + dz) % 4) + yh, "col": 2 * x + k} for dz in (1, 2, 3)]
     pass_on = [{"row": row, "col": 2 * ((z + dz) % 4) + yh} for dz in (1, 2, 3)]
+    apart = (x - z + 4) % 4
+    near_by = apart % 2 == 1
+    far_off = apart == 2
+    hop_out = {"row": 2 * ((z + jnp.where(x % 2 == SIDE, 1, 3)) % 4) + yh, "col": 2 * x + k}
+    hop_in = {"row": 2 * ((x + jnp.where(z % 2 == SIDE, 1, 3)) % 4) + k, "col": 2 * z + yh}
+    hop_from = {"row": 2 * ((x + 2) % 4) + yh, "col": 2 * x + k}
+    hop_to = {"row": 2 * x + k, "col": 2 * ((x + 2) % 4) + yh}
+    helps = apart == jnp.where(x % 2 == SIDE, 1, 3)
 
     barrier = pltpu.get_barrier_semaphore()
 
@@ -95,17 +104,25 @@
 
     greet([to_layer, to_y, to_core, *to_x, *to_z])
 
-    @pl.when(crossed)
+    @pl.when(jnp.logical_and(crossed, jnp.logical_not(far_off)))
     def _():
         greet([to_crossed])
 
     @pl.when(on_ring)
     def _():
-        greet(pass_from + pass_on)
-
-    @pl.when(jnp.logical_not(on_ring))
+        greet([pass_from[0], pass_from[2], pass_on[0], pass_on[2]])
+
+    @pl.when(near_by)
     def _():
         greet([to_straight, pass_out, pass_in])
+
+    @pl.when(helps)
+    def _():
+        greet([hop_from, hop_to])
+
+    @pl.when(far_off)
+    def _():
+        greet([hop_out, hop_in])
 
     def copy(source, target, send, recv, device):
         return pltpu.make_async_remote_copy(
@@ -160,6 +177,18 @@
             mirror_out.at[mirror_part(1, ch)], passing.at[slot, at], mirror_s.at[1, ch], pass_r.at[slot, ch], pass_from[slot]
         )
 
+    def hop_copy(p, ch):
+        at = pl.ds(ch * sub, sub)
+        return copy(
+            mirror_out.at[mirror_part(p, ch)], passing.at[p, at], mirror_s.at[p, ch], pass_r.at[p, ch], hop_out
+        )
+
+    def hop_on(p, ch):
+        at = pl.ds(ch * sub, sub)
+        return copy(
+            passing.at[p, at], mirror_in.at[mirror_part(p, ch)], pass_s.at[p, ch], mirror_r.at[p, ch], hop_to
+        )
+
     def layer_copy(ch):
         at = part(lay, ch)
         return copy(same0.at[at], same0.at[at], layer_s.at[ch], layer_r.at[ch], to_layer)
@@ -171,19 +200,28 @@
         slot = (6 if way == 0 else 2) + s
         return copy(left.at[s, piece(ch)], left.at[slot, piece(ch)], x_s.at[way, s, ch], x_r.at[way, s, ch], to_x[way])
 
-    def x_forward(way, ch):
-        slot = 6 if way == 0 else 3
-        return copy(left.at[slot, piece(ch)], left.at[4 + way, piece(ch)], xf_s.at[way, ch], xf_r.at[way, ch], to_x[way])
+    def x_forward(way, s, ch):
+        slot = (6 if way == 0 else 2) + s
+        return copy(left.at[slot, piece(ch)], left.at[4 + s, piece(ch)], xf_s.at[s, ch], xf_r.at[s, ch], to_x[way])
 
     def z_copy(way, d, ch):
         at = part(half_of(d), ch)
         target = same3 if way == 0 else same1
         return copy(same0.at[at], target.at[at], z_s.at[way, d, ch], z_r.at[way, d, ch], to_z[way])
 
-    def z_forward(way, ch):
-        at = part(half_of(way), ch)
+    def z_forward(way, d, ch):
+        at = part(half_of(d), ch)
         source = same3 if way == 0 else same1
-        return copy(source.at[at], same2.at[at], zf_s.at[way, ch], zf_r.at[way, ch], to_z[way])
+        return copy(source.at[at], same2.at[at], zf_s.at[d, ch], zf_r.at[d, ch], to_z[way])
+
+    def one_way(ch, start):
+        @pl.when(ch < CHUNKS // 2)
+        def _():
+            start(0)
+
+        @pl.when(ch >= CHUNKS // 2)
+        def _():
+            start(1)
 
     def core_copy(dz, d, ch):
         at = part(half_of(d), ch)
@@ -196,7 +234,9 @@
 
         lax.fori_loop(0, CHUNKS, run, 0)
 
-    pl.semaphore_wait(barrier, 7 + jnp.where(on_ring, 6, 3) + jnp.where(crossed, 1, 0))
+    greeted = jnp.where(on_ring, 4, jnp.where(far_off, 2, 3)) + jnp.where(helps, 2, 0)
+    greeted += jnp.where(jnp.logical_and(crossed, jnp.logical_not(far_off)), 1, 0)
+    pl.semaphore_wait(barrier, 7 + greeted)
 
     def send_mirrored(ch):
         def pick(n, carry):
@@ -212,7 +252,12 @@
             mirror_copy(0, ch, to_crossed).start()
             mirror_copy(1, ch, to_crossed).start()
 
-        @pl.when(jnp.logical_not(on_ring))
+        @pl.when(far_off)
+        def _():
+            hop_copy(0, ch).start()
+            hop_copy(1, ch).start()
+
+        @pl.when(near_by)
         def _():
             @pl.when(crossed)
             def _():
@@ -234,16 +279,24 @@
 
     lax.fori_loop(0, half, clear, 0)
 
-    def straight_on(ch):
-        swap_copy(ch).wait_recv()
-        swap_on(ch).start()
-
-    @pl.when(jnp.logical_and(crossed, jnp.logical_not(on_ring)))
-    def _():
-        each(straight_on)
+    def send_on(ch):
+        @pl.when(crossed)
+        def _():
+            swap_copy(ch).wait_recv()
+            swap_on(ch).start()
+
+        @pl.when(helps)
+        def _():
+            for p in range(2):
+                hop_copy(p, ch).wait_recv()
+                hop_on(p, ch).start()
+
+    @pl.when(near_by)
+    def _():
+        each(send_on)
 
     def pass_along(ch):
-        for slot in range(3):
+        for slot in (0, 2):
             arriving(slot, ch).wait_recv()
             passing_copy(slot, ch).start()
 
@@ -288,43 +341,46 @@
 
     each(complete)
 
-    def spread(ch):
+    def spread_layer(ch):
         layer_copy(ch).wait_recv()
         y_copy(ch).start()
         for way in range(2):
             z_copy(way, 1, ch).start()
         core_copy(0, 1, ch).start()
+
+    each(spread_layer)
+
+    def forward_own(ch):
+        for way in range(2):
+            x_copy(way, 0, ch).wait_recv()
+        one_way(ch, lambda way: x_forward(way, 0, ch).start())
+        for way in range(2):
+            z_copy(way, 0, ch).wait_recv()
+        one_way(ch, lambda way: z_forward(way, 0, ch).start())
+        for dz in (1, 3):
+            core_copy(dz, 0, ch).start()
+
+    def spread_y(ch):
         y_copy(ch).wait_recv()
         for way in range(2):
             x_copy(way, 1, ch).start()
 
-    each(spread)
-
-    def forward_first(ch):
-        x_copy(0, 0, ch).wait_recv()
-        x_forward(0, ch).start()
-        z_copy(0, 0, ch).wait_recv()
-        z_forward(0, ch).start()
-        core_copy(3, 0, ch).start()
-        z_copy(1, 0, ch).wait_recv()
-        core_copy(1, 0, ch).start()
-
-    each(forward_first)
+    each(spread_y)
+    each(forward_own)
 
     def forward_second(ch):
-        x_copy(1, 1, ch).wait_recv()
-        x_forward(1, ch).start()
-        z_copy(1, 1, ch).wait_recv()
-        z_forward(1, ch).start()
-        core_copy(1, 1, ch).start()
-        z_copy(0, 1, ch).wait_recv()
-        core_copy(3, 1, ch).start()
+        for way in range(2):
+            x_copy(way, 1, ch).wait_recv()
+        one_way(ch, lambda way: x_forward(way, 1, ch).start())
+        for way in range(2):
+            z_copy(way, 1, ch).wait_recv()
+        one_way(ch, lambda way: z_forward(way, 1, ch).start())
+        for dz in (1, 3):
+            core_copy(dz, 1, ch).start()
 
     each(forward_second)
 
     def near(ch):
-        x_copy(1, 0, ch).wait_recv()
-        x_copy(0, 1, ch).wait_recv()
         for dz in (0, 1, 3):
             for d in range(2):
                 core_copy(dz, d, ch).wait_recv()
@@ -360,10 +416,10 @@
             multiply(dz, 1)
 
     def last(ch):
-        for way in range(2):
-            z_forward(way, ch).wait_recv()
-            core_copy(2, way, ch).start()
-            x_forward(way, ch).wait_recv()
+        for d in range(2):
+            z_forward(0, d, ch).wait_recv()
+            core_copy(2, d, ch).start()
+            x_forward(0, d, ch).wait_recv()
 
     each(last)
 
@@ -388,20 +444,25 @@
             mirror_copy(0, ch, to_straight).wait_send()
             mirror_copy(1, ch, to_straight).wait_send()
 
-        @pl.when(jnp.logical_and(crossed, jnp.logical_not(on_ring)))
+        @pl.when(jnp.logical_and(crossed, near_by))
         def _():
             swap_on(ch).wait_send()
 
         @pl.when(on_ring)
         def _():
-            for slot in range(3):
+            for slot in (0, 2):
                 passing_copy(slot, ch).wait_send()
+
+        @pl.when(helps)
+        def _():
+            for p in range(2):
+                hop_on(p, ch).wait_send()
 
         layer_copy(ch).wait_send()
         y_copy(ch).wait_send()
         for way in range(2):
-            x_forward(way, ch).wait_send()
-            z_forward(way, ch).wait_send()
+            x_forward(0, way, ch).wait_send()
+            z_forward(0, way, ch).wait_send()
             for d in range(2):
                 x_copy(way, d, ch).wait_send()
                 z_copy(way, d, ch).wait_send()

time: 172 us -> 166 us (0.965)
  the two profiles are of different devices: /device:TPU:40 before, /device:TPU:10 now
where the time goes in v4:
time: 166 us
  Pallas kernels  162 us (98%)
  local copies, waits for them, and re-layouts  3.91 us (2%)
    pallas_call x1, Pallas kernels, per_device(): pl.pallas_call(functools.partial(kernel, rows), out_shape=jax.ShapeDtypeS...  162 us
    unnamed x1, local copies, waits for them, and re-layouts  3.91 us

profile of v4, /device:TPU:10, one launch (start us, length us, event | category | flops | bytes accessed | tf_op | source)
XLA Modules:
  0.0 165.8 jit_solution(15402455431032108671)
XLA Ops:
  0.0 161.9 %shard_map.37 = f32[24,2,128,128]{3,2,1,0:T(8,128)} custom-call(s32[8,8,48]{2,1,0:T(8,128)} %pattern.1, s32[2,48]{1,0:T(2,128)} %bitcast.7, f32[48,128,128]{2,1,0:T(8,128)} %bitcast.6), custom_call_target="tpu_custom_call" | custom-call | tf_op jit(solution)/shard_map/pallas_call | solution.py:484
  161.9 3.9 %copy.5 = f32[1,1,24,2,128,128]{5,4,3,2,1,0:T(8,128)} copy(f32[1,1,24,2,128,128]{5,4,3,2,1,0:T(8,128)} %bitcast.5) | data formatting | bytes 6291456

commit v5 on v4

--- a/solution.py
+++ b/solution.py
@@ -53,6 +53,10 @@
     y_r,
     x_s,
     x_r,
+    pair_s,
+    pair_r,
+    side_s,
+    side_r,
     xf_s,
     xf_r,
     z_s,
@@ -78,6 +82,7 @@
 
     to_layer = {"layer": 1 - lay}
     to_y = {"col": 2 * x + (1 - yh), "layer": 1 - lay}
+    to_pair = {"col": 2 * x + (1 - yh)}
     to_core = {"row": 2 * z + (1 - k)}
     to_x = [{"col": (col + 2) % 8}, {"col": (col + 6) % 8}]
     to_z = [{"row": (row + 2) % 8}, {"row": (row + 6) % 8}]
@@ -102,7 +107,7 @@
         for device in devices:
             pl.semaphore_signal(barrier, inc=1, device_id=device, device_id_type=MESH)
 
-    greet([to_layer, to_y, to_core, *to_x, *to_z])
+    greet([to_layer, to_y, to_pair, to_core, *to_x, *to_z])
 
     @pl.when(jnp.logical_and(crossed, jnp.logical_not(far_off)))
     def _():
@@ -200,6 +205,23 @@
         slot = (6 if way == 0 else 2) + s
         return copy(left.at[s, piece(ch)], left.at[slot, piece(ch)], x_s.at[way, s, ch], x_r.at[way, s, ch], to_x[way])
 
+    aside = (CHUNKS - 1, 0)
+
+    def kept(way, ch, act):
+        @pl.when(ch != aside[way])
+        def _():
+            act()
+
+    def pair_copy(way):
+        slot = 6 if way == 0 else 2
+        at = piece(aside[way])
+        return copy(left.at[slot, at], left.at[slot + 1, at], pair_s.at[way], pair_r.at[way], to_pair)
+
+    def side_copy(way):
+        tile = same3 if way == 0 else same1
+        at = part(lay, aside[way])
+        return copy(tile.at[at], tile.at[at], side_s.at[way], side_r.at[way], to_layer)
+
     def x_forward(way, s, ch):
         slot = (6 if way == 0 else 2) + s
         return copy(left.at[slot, piece(ch)], left.at[4 + s, piece(ch)], xf_s.at[s, ch], xf_r.at[s, ch], to_x[way])
@@ -236,7 +258,7 @@
 
     greeted = jnp.where(on_ring, 4, jnp.where(far_off, 2, 3)) + jnp.where(helps, 2, 0)
     greeted += jnp.where(jnp.logical_and(crossed, jnp.logical_not(far_off)), 1, 0)
-    pl.semaphore_wait(barrier, 7 + greeted)
+    pl.semaphore_wait(barrier, 8 + greeted)
 
     def send_mirrored(ch):
         def pick(n, carry):
@@ -345,7 +367,7 @@
         layer_copy(ch).wait_recv()
         y_copy(ch).start()
         for way in range(2):
-            z_copy(way, 1, ch).start()
+            kept(way, ch, z_copy(way, 1, ch).start)
         core_copy(0, 1, ch).start()
 
     each(spread_layer)
@@ -359,26 +381,35 @@
         one_way(ch, lambda way: z_forward(way, 0, ch).start())
         for dz in (1, 3):
             core_copy(dz, 0, ch).start()
+        for way in range(2):
+            @pl.when(ch == aside[way])
+            def _(way=way):
+                side_copy(way).start()
+                pair_copy(way).start()
 
     def spread_y(ch):
         y_copy(ch).wait_recv()
         for way in range(2):
-            x_copy(way, 1, ch).start()
+            kept(way, ch, x_copy(way, 1, ch).start)
 
     each(spread_y)
     each(forward_own)
 
     def forward_second(ch):
         for way in range(2):
-            x_copy(way, 1, ch).wait_recv()
+            kept(way, ch, x_copy(way, 1, ch).wait_recv)
         one_way(ch, lambda way: x_forward(way, 1, ch).start())
         for way in range(2):
-            z_copy(way, 1, ch).wait_recv()
+            kept(way, ch, z_copy(way, 1, ch).wait_recv)
         one_way(ch, lambda way: z_forward(way, 1, ch).start())
-        for dz in (1, 3):
-            core_copy(dz, 1, ch).start()
+        for way, dz in ((0, 3), (1, 1)):
+            kept(way, ch, core_copy(dz, 1, ch).start)
 
     each(forward_second)
+    for way, dz in ((0, 3), (1, 1)):
+        side_copy(way).wait_recv()
+        core_copy(dz, 1, aside[way]).start()
+        pair_copy(way).wait_recv()
 
     def near(ch):
         for dz in (0, 1, 3):
@@ -463,14 +494,18 @@
         for way in range(2):
             x_forward(0, way, ch).wait_send()
             z_forward(0, way, ch).wait_send()
-            for d in range(2):
-                x_copy(way, d, ch).wait_send()
-                z_copy(way, d, ch).wait_send()
+            x_copy(way, 0, ch).wait_send()
+            z_copy(way, 0, ch).wait_send()
+            kept(way, ch, x_copy(way, 1, ch).wait_send)
+            kept(way, ch, z_copy(way, 1, ch).wait_send)
         for dz in range(4):
             for d in range(2):
                 core_copy(dz, d, ch).wait_send()
 
     each(drain)
+    for way in range(2):
+        side_copy(way).wait_send()
+        pair_copy(way).wait_send()
 
 
 def per_device(stored_blocks, pattern, result_cols):
@@ -498,6 +533,7 @@
             *[sems((3, CHUNKS))] * 2,
             *[sems((CHUNKS,))] * 4,
             *[sems((2, 2, CHUNKS))] * 2,
+            *[sems((2,))] * 4,
             *[sems((2, CHUNKS))] * 2,
             *[sems((2, 2, CHUNKS))] * 2,
             *[sems((2, CHUNKS))] * 2,

time: 166 us -> 158 us (0.952)
  Pallas kernels: 162 us -> 154 us
    pallas_call x1, Pallas kernels: 162 us -> 154 us  [per_device(): pl.pallas_call(functools.partial(kernel, rows), out_shape=jax.ShapeDtypeS...]
where the time goes in v5:
time: 158 us; the launch traced here: 157 us
  Pallas kernels  154 us (97%)
  local copies, waits for them, and re-layouts  3.91 us (2%)
    pallas_call x1, Pallas kernels, per_device(): pl.pallas_call(functools.partial(kernel, rows), out_shape=jax.ShapeDtypeS...  154 us
    unnamed x1, local copies, waits for them, and re-layouts  3.91 us

profile of v5, /device:TPU:10, one launch (start us, length us, event | category | flops | bytes accessed | tf_op | source)
XLA Modules:
  0.0 157.5 jit_solution(3878201265411982165)
XLA Ops:
  0.0 153.5 %shard_map.37 = f32[24,2,128,128]{3,2,1,0:T(8,128)} custom-call(s32[8,8,48]{2,1,0:T(8,128)} %pattern.1, s32[2,48]{1,0:T(2,128)} %bitcast.7, f32[48,128,128]{2,1,0:T(8,128)} %bitcast.6), custom_call_target="tpu_custom_call" | custom-call | tf_op jit(solution)/shard_map/pallas_call | solution.py:519
  153.5 3.9 %copy.5 = f32[1,1,24,2,128,128]{5,4,3,2,1,0:T(8,128)} copy(f32[1,1,24,2,128,128]{5,4,3,2,1,0:T(8,128)} %bitcast.5) | data formatting | bytes 6291456

commit v6 on v5

--- a/solution.py
+++ b/solution.py
@@ -8,7 +8,8 @@
 from jax.sharding import PartitionSpec as P
 
 MESH = pl.DeviceIdType.MESH
-CHUNKS = 4
+CHUNKS = 6
+ASIDE = 2
 SIDE = 0
 
 
@@ -26,8 +27,10 @@
     rows,
     pattern,
     wanted,
+    stored_hbm,
+    out,
     stored,
-    out,
+    stored_sem,
     mirror_out,
     mirror_in,
     swapped,
@@ -101,6 +104,8 @@
     hop_to = {"row": 2 * x + k, "col": 2 * ((x + 2) % 4) + yh}
     helps = apart == jnp.where(x % 2 == SIDE, 1, 3)
 
+    load = pltpu.make_async_copy(stored_hbm, stored, stored_sem)
+    load.start()
     barrier = pltpu.get_barrier_semaphore()
 
     def greet(devices):
@@ -205,21 +210,21 @@
         slot = (6 if way == 0 else 2) + s
         return copy(left.at[s, piece(ch)], left.at[slot, piece(ch)], x_s.at[way, s, ch], x_r.at[way, s, ch], to_x[way])
 
-    aside = (CHUNKS - 1, 0)
+    aside = (CHUNKS - ASIDE, 0)
 
     def kept(way, ch, act):
-        @pl.when(ch != aside[way])
+        @pl.when(ch < aside[0] if way == 0 else ch >= ASIDE)
         def _():
             act()
 
     def pair_copy(way):
         slot = 6 if way == 0 else 2
-        at = piece(aside[way])
+        at = pl.ds(aside[way] * step, ASIDE * step)
         return copy(left.at[slot, at], left.at[slot + 1, at], pair_s.at[way], pair_r.at[way], to_pair)
 
     def side_copy(way):
         tile = same3 if way == 0 else same1
-        at = part(lay, aside[way])
+        at = pl.ds(lay * half + aside[way] * step, ASIDE * step)
         return copy(tile.at[at], tile.at[at], side_s.at[way], side_r.at[way], to_layer)
 
     def x_forward(way, s, ch):
@@ -259,6 +264,8 @@
     greeted = jnp.where(on_ring, 4, jnp.where(far_off, 2, 3)) + jnp.where(helps, 2, 0)
     greeted += jnp.where(jnp.logical_and(crossed, jnp.logical_not(far_off)), 1, 0)
     pl.semaphore_wait(barrier, 8 + greeted)
+
+    load.wait()
 
     def send_mirrored(ch):
         def pick(n, carry):
@@ -382,7 +389,7 @@
         for dz in (1, 3):
             core_copy(dz, 0, ch).start()
         for way in range(2):
-            @pl.when(ch == aside[way])
+            @pl.when(ch == aside[way] + ASIDE - 1)
             def _(way=way):
                 side_copy(way).start()
                 pair_copy(way).start()
@@ -408,7 +415,8 @@
     each(forward_second)
     for way, dz in ((0, 3), (1, 1)):
         side_copy(way).wait_recv()
-        core_copy(dz, 1, aside[way]).start()
+        for n in range(ASIDE):
+            core_copy(dz, 1, aside[way] + n).start()
         pair_copy(way).wait_recv()
 
     def near(ch):
@@ -435,7 +443,7 @@
                 out[n, q] += block * jnp.where(matched, 1.0, 0.0)
             return carry
 
-        lax.fori_loop(0, half, one, 0, unroll=4)
+        lax.fori_loop(0, half, one, 0, unroll=8)
 
     def far(dz):
         return (z + dz - x + 4) % 4 == 2
@@ -519,9 +527,11 @@
     result = pl.pallas_call(
         functools.partial(kernel, rows),
         out_shape=jax.ShapeDtypeStruct((half, 2, *block), jnp.float32),
-        in_specs=[smem, smem, vmem],
+        in_specs=[smem, smem, pl.BlockSpec(memory_space=pl.ANY)],
         out_specs=vmem,
         scratch_shapes=[
+            pltpu.VMEM((rows, *block), jnp.float32),
+            sems(()),
             pltpu.VMEM((half, *block), jnp.float32),
             pltpu.VMEM((half, *block), jnp.float32),
             pltpu.VMEM((half // 2, *block), jnp.float32),

time: 158 us -> 152 us (0.962)
  Pallas kernels: 154 us -> 147 us
    pallas_call x1, Pallas kernels: 154 us -> 147 us  [per_device(): pl.pallas_call(functools.partial(kernel, rows), out_shape=jax.ShapeDtypeS...]
where the time goes in v6:
time: 152 us; the launch traced here: 151 us
  Pallas kernels  147 us (97%)
  local copies, waits for them, and re-layouts  3.91 us (3%)
    pallas_call x1, Pallas kernels, per_device(): pl.pallas_call(functools.partial(kernel, rows), out_shape=jax.ShapeDtypeS...  147 us
    unnamed x1, local copies, waits for them, and re-layouts  3.91 us

profile of v6, /device:TPU:10, one launch (start us, length us, event | category | flops | bytes accessed | tf_op | source)
XLA Modules:
  0.0 150.8 jit_solution(1110588612406413235)
XLA Ops:
  0.0 146.9 %shard_map.37 = f32[24,2,128,128]{3,2,1,0:T(8,128)} custom-call(s32[8,8,48]{2,1,0:T(8,128)} %pattern.1, s32[2,48]{1,0:T(2,128)} %bitcast.7, f32[48,128,128]{2,1,0:T(8,128)} %bitcast.6), custom_call_target="tpu_custom_call" | custom-call | tf_op jit(solution)/shard_map/pallas_call | solution.py:527
  146.9 3.9 %copy.5 = f32[1,1,24,2,128,128]{5,4,3,2,1,0:T(8,128)} copy(f32[1,1,24,2,128,128]{5,4,3,2,1,0:T(8,128)} %bitcast.5) | data formatting | bytes 6291456

commit v7 on v6

--- a/solution.py
+++ b/solution.py
@@ -10,6 +10,7 @@
 MESH = pl.DeviceIdType.MESH
 CHUNKS = 6
 ASIDE = 2
+DIRECT = 2
 SIDE = 0
 
 
@@ -98,6 +99,7 @@
     apart = (x - z + 4) % 4
     near_by = apart % 2 == 1
     far_off = apart == 2
+    to_mirror = {"row": col, "col": row}
     hop_out = {"row": 2 * ((z + jnp.where(x % 2 == SIDE, 1, 3)) % 4) + yh, "col": 2 * x + k}
     hop_in = {"row": 2 * ((x + jnp.where(z % 2 == SIDE, 1, 3)) % 4) + k, "col": 2 * z + yh}
     hop_from = {"row": 2 * ((x + 2) % 4) + yh, "col": 2 * x + k}
@@ -132,7 +134,7 @@
 
     @pl.when(far_off)
     def _():
-        greet([hop_out, hop_in])
+        greet([hop_out, hop_in, to_mirror])
 
     def copy(source, target, send, recv, device):
         return pltpu.make_async_remote_copy(
@@ -187,6 +189,9 @@
             mirror_out.at[mirror_part(1, ch)], passing.at[slot, at], mirror_s.at[1, ch], pass_r.at[slot, ch], pass_from[slot]
         )
 
+    def by_hops(ch):
+        return ch < CHUNKS - DIRECT
+
     def hop_copy(p, ch):
         at = pl.ds(ch * sub, sub)
         return copy(
@@ -261,7 +266,7 @@
 
         lax.fori_loop(0, CHUNKS, run, 0)
 
-    greeted = jnp.where(on_ring, 4, jnp.where(far_off, 2, 3)) + jnp.where(helps, 2, 0)
+    greeted = jnp.where(on_ring, 4, 3) + jnp.where(helps, 2, 0)
     greeted += jnp.where(jnp.logical_and(crossed, jnp.logical_not(far_off)), 1, 0)
     pl.semaphore_wait(barrier, 8 + greeted)
 
@@ -281,10 +286,15 @@
             mirror_copy(0, ch, to_crossed).start()
             mirror_copy(1, ch, to_crossed).start()
 
-        @pl.when(far_off)
+        @pl.when(jnp.logical_and(far_off, by_hops(ch)))
         def _():
             hop_copy(0, ch).start()
             hop_copy(1, ch).start()
+
+        @pl.when(jnp.logical_and(far_off, jnp.logical_not(by_hops(ch))))
+        def _():
+            mirror_copy(0, ch, to_mirror).start()
+            mirror_copy(1, ch, to_mirror).start()
 
         @pl.when(near_by)
         def _():
@@ -314,7 +324,7 @@
             swap_copy(ch).wait_recv()
             swap_on(ch).start()
 
-        @pl.when(helps)
+        @pl.when(jnp.logical_and(helps, by_hops(ch)))
         def _():
             for p in range(2):
                 hop_copy(p, ch).wait_recv()
@@ -492,7 +502,7 @@
             for slot in (0, 2):
                 passing_copy(slot, ch).wait_send()
 
-        @pl.when(helps)
+        @pl.when(jnp.logical_and(helps, by_hops(ch)))
         def _():
             for p in range(2):
                 hop_on(p, ch).wait_send()

time: 152 us -> 151 us (level)
  the two profiles are of different devices: /device:TPU:10 before, /device:TPU:5 now
where the time goes in v7:
time: 151 us; the launch traced here: 150 us
  Pallas kernels  147 us (97%)
  local copies, waits for them, and re-layouts  3.91 us (3%)
    pallas_call x1, Pallas kernels, per_device(): pl.pallas_call(functools.partial(kernel, rows), out_shape=jax.ShapeDtypeS...  147 us
    unnamed x1, local copies, waits for them, and re-layouts  3.91 us

profile of v7, /device:TPU:5, one launch (start us, length us, event | category | flops | bytes accessed | tf_op | source)
XLA Modules:
  0.0 150.5 jit_solution(9400933043309314641)
XLA Ops:
  0.0 146.6 %shard_map.37 = f32[24,2,128,128]{3,2,1,0:T(8,128)} custom-call(s32[8,8,48]{2,1,0:T(8,128)} %pattern.1, s32[2,48]{1,0:T(2,128)} %bitcast.7, f32[48,128,128]{2,1,0:T(8,128)} %bitcast.6), custom_call_target="tpu_custom_call" | custom-call | tf_op jit(solution)/shard_map/pallas_call | solution.py:537
  146.6 3.9 %copy.5 = f32[1,1,24,2,128,128]{5,4,3,2,1,0:T(8,128)} copy(f32[1,1,24,2,128,128]{5,4,3,2,1,0:T(8,128)} %bitcast.5) | data formatting | bytes 6291456
